TPU v7x, 32 devices: a whole 2x2x4 slice. The times are simulated.
32 devices in a mesh: parts: 2 (over y), expert: 4 (over z), dp: 2 (over x), tensor: 2 (over core).
Axes of the slice: x: 2, y: 2, z: 4, core: 2. Of those that a mesh axis runs over, the one named last changes fastest.
Arguments:
- tokens: bfloat16 [4096, 7168], P(('parts', 'expert', 'tensor'), 'dp'), parts along dimension 0, may hold values from -6 to 6
- cotangent: bfloat16 [4096, 7168], P(('parts', 'expert', 'tensor'), 'dp'), parts along dimension 0, may hold values from -0.59765625 to 0.59765625
- norm_gain: float32 [7168], P('dp'), may hold values from 0.5 to 1.5
- expert_ids: int32 [4096, 1], P(('parts', 'expert', 'tensor')), parts along dimension 0, may hold values from 0 to 1; in each aligned block of 256 rows (0 to 255, 256 to 511, ...) at most 160 rows name the same one
- combine_weight: float32 [4096], P(('parts', 'expert', 'tensor')), parts along dimension 0, may hold values from 0.2 to 1
- up_weight: bfloat16 [7168, 2048], P('dp', ('expert', 'tensor')), may hold values from -0.0625 to 0.0625
- down_weight: bfloat16 [2048, 7168], P(('expert', 'tensor'), 'dp'), may hold values from -0.1875 to 0.1875
Outputs:
- token_grad: bfloat16 [4096, 7168], P(('parts', 'expert', 'tensor'), 'dp'), parts along dimension 0
- up_grad: bfloat16 [14336, 2048], P(('parts', 'dp'), ('expert', 'tensor')), parts along dimension 0
- down_grad: bfloat16 [4096, 7168], P(('parts', 'expert', 'tensor'), 'dp'), parts along dimension 0
- gain_grad: float32 [14336], P(('parts', 'dp')), parts along dimension 0
- token_inner: float32 [4096], P(('parts', 'expert', 'tensor')), parts along dimension 0
There are 2 independent parts, one for each index of `parts`. A program takes and returns all parts, laid end to end along the dimension named above; an argument that names none is the same for every part. Nothing has to cross between parts.
Inputs may be any that keep to these rules, and one draw needn't show every extreme that they name: `expert_ids`: each row names one routed expert. Within the rows of one device (aligned blocks of 256 rows) no expert is named by more than 160 rows, a bound that some block reaches.
All inputs are finite; a program needn't handle non-finite values.
Results may differ from a plain program's by a relative error of at most 0.014.
Values may be sent and summed in bfloat16 or wider, within the bound.
A program may use at most 128 MiB of HBM per device.

v0:
```python
import jax
import jax.numpy as jnp
from jax import lax
from jax.sharding import PartitionSpec as P


def slope(pre):
    sig = jax.nn.sigmoid(pre)
    return sig * (1.0 + pre * (1.0 - sig))


def contract(left, right, left_dim, right_dim):
    return lax.dot_general(
        left, right, (((left_dim,), (right_dim,)), ((), ())), preferred_element_type=jnp.float32
    )


def local(tokens, cotangent, norm_gain, expert_ids, combine_weight, up_weight, down_weight):
    n_expert = lax.axis_size("expert")
    groups = n_expert // 2
    count, piece = tokens.shape
    width = piece * lax.axis_size("dp")
    capacity = count * 5 // (4 * groups)
    token_f = tokens.astype(jnp.float32)
    squares = lax.psum(jnp.sum(token_f * token_f, axis=1, keepdims=True), "dp")
    scale = lax.rsqrt(squares / width + 1e-06)
    normed = (token_f * scale * norm_gain[None, :]).astype(jnp.bfloat16)
    scaled = (combine_weight[:, None] * cotangent.astype(jnp.float32)).astype(jnp.bfloat16)
    target = expert_ids[:, 0]
    hits = (target[:, None] == jnp.arange(groups, dtype=jnp.int32)[None, :]).astype(jnp.int32)
    slot = jnp.sum((jnp.cumsum(hits, axis=0) - 1) * hits, axis=1)
    flat_slot = target * capacity + slot
    places = (flat_slot[:, None] == jnp.arange(groups * capacity, dtype=jnp.int32)[None, :]).astype(
        jnp.bfloat16
    )
    packed_x = contract(places, normed, 0, 0).astype(jnp.bfloat16)
    packed_d = contract(places, scaled, 0, 0).astype(jnp.bfloat16)

    def outward(packed):
        return jnp.repeat(packed.reshape(groups, capacity, piece), 2, axis=0)

    sent_x, sent_d = (
        lax.all_to_all(outward(packed_x), "expert", split_axis=0, concat_axis=0, tiled=True),
        lax.all_to_all(outward(packed_d), "expert", split_axis=0, concat_axis=0, tiled=True),
    )
    rows_x = sent_x.reshape(-1, piece)
    rows_d = sent_d.reshape(-1, piece)
    full_up, full_down = (
        lax.all_gather(up_weight, "tensor", axis=1, tiled=True),
        lax.all_gather(down_weight, "tensor", axis=0, tiled=True),
    )
    up_part = jnp.dot(rows_x, full_up, preferred_element_type=jnp.float32)
    back_part = contract(rows_d, full_down, 1, 1)
    pre, back = (
        lax.psum(up_part.astype(jnp.bfloat16), "dp").astype(jnp.float32),
        lax.psum(back_part.astype(jnp.bfloat16), "dp").astype(jnp.float32),
    )
    act = jax.nn.silu(pre).astype(jnp.bfloat16)
    dpre = (back * slope(pre)).astype(jnp.bfloat16)
    down_terms = contract(act, rows_d, 0, 0)
    up_terms = contract(rows_x, dpre, 0, 0)
    down_sum, up_sum = (
        lax.psum_scatter(
            down_terms.astype(jnp.bfloat16), "tensor", scatter_dimension=0, tiled=True
        ).astype(jnp.float32),
        lax.psum_scatter(
            up_terms.astype(jnp.bfloat16), "tensor", scatter_dimension=1, tiled=True
        ).astype(jnp.float32),
    )
    down_grad = down_sum.astype(jnp.bfloat16)
    up_grad = up_sum.astype(jnp.bfloat16)
    row_grad = contract(dpre, full_up, 1, 1).astype(jnp.bfloat16)
    returned = lax.all_to_all(
        row_grad.reshape(n_expert, capacity, piece),
        "expert",
        split_axis=0,
        concat_axis=0,
        tiled=True,
    )
    returned = returned.reshape(groups, 2, capacity, piece).astype(jnp.float32)
    merged = (returned[:, 0] + returned[:, 1]).reshape(groups * capacity, piece)
    normed_grad = jnp.take(merged, flat_slot, axis=0)
    gain_terms = jnp.sum(normed_grad * token_f * scale, axis=0)
    gain_grad = lax.psum(gain_terms, ("expert", "tensor"))
    inner_part = jnp.sum(token_f * norm_gain[None, :] * normed_grad, axis=1, keepdims=True)
    inner = lax.psum(inner_part, "dp")
    cubed = scale * scale * scale
    token_grad = (
        cotangent.astype(jnp.float32)
        + scale * norm_gain[None, :] * normed_grad
        - token_f * cubed * inner / width
    )
    return (token_grad.astype(jnp.bfloat16), up_grad, down_grad, gain_grad, inner[:, 0])


def solution(mesh):
    in_specs = (
        P(("parts", "expert", "tensor"), "dp"),
        P(("parts", "expert", "tensor"), "dp"),
        P("dp"),
        P(("parts", "expert", "tensor"), None),
        P(("parts", "expert", "tensor")),
        P("dp", ("expert", "tensor")),
        P(("expert", "tensor"), "dp"),
    )
    out_specs = (
        P(("parts", "expert", "tensor"), "dp"),
        P(("parts", "dp"), ("expert", "tensor")),
        P(("parts", "expert", "tensor"), "dp"),
        P(("parts", "dp")),
        P(("parts", "expert", "tensor")),
    )
    return jax.shard_map(local, mesh=mesh, in_specs=in_specs, out_specs=out_specs, check_vma=False)
```

profile of v0, /device:TPU:0, one launch (start us, length us, event | category | flops | bytes accessed | tf_op | source)
XLA Modules:
  0.0 469.5 jit_solution(201301883073382467)
XLA Ops:
  10.3 2.4 convolution_convert_fusion.4
  12.7 2.5 broadcast_in_dim.31
  15.3 6.5 %all-to-all-start = ((bf16[4,160,3584]{2,1,0:T(8,128)(2,1)}), bf16[4,160,3584]{2,1,0:T(8,128)(2,1)}, u32[]{:S(2)}, u32[]{:S(2)}) async-start(bf16[4,160,3584]{2,1,0:T(8,128)(2,1)} %bitcast.46), calls=%async_computation | async-start | bytes 9175040 | tf_op jit(solution)/shard_map/all_to_all | solution.py:44
  22.9 4.9 %psum.35 = f32[256,1]{0,1:T(1,128)S(1)} all-reduce(f32[256,1]{0,1:T(1,128)S(1)} %bitcast.58), channel_id=1, replica_groups=mesh['parts'=2,'expert'=4,'dp'=2,'tensor'=2] {'dp'}, use_global_device_ids=true, to_apply=%region_1.0 | all-reduce | flops 256 | bytes 2048 | tf_op jit(solution)/shard_map/psum | solution.py:25
  30.2 93.5 %all-to-all-done = bf16[4,160,3584]{2,1,0:T(8,128)(2,1)} async-done(((bf16[4,160,3584]{2,1,0:T(8,128)(2,1)}), bf16[4,160,3584]{2,1,0:T(8,128)(2,1)}, u32[]{:S(2)}, u32[]{:S(2)}) %all-to-all-start) | async-done | bytes 4587552 | tf_op jit(solution)/shard_map/all_to_all | solution.py:44
  123.6 4.2 broadcast_in_dim.32
  127.8 4.9 %all-to-all-start.1 = ((bf16[4,160,3584]{2,1,0:T(8,128)(2,1)}), bf16[4,160,3584]{2,1,0:T(8,128)(2,1)}, u32[]{:S(2)}, u32[]{:S(2)}) async-start(bf16[4,160,3584]{2,1,0:T(8,128)(2,1)} %bitcast.45), calls=%async_computation.1 | async-start | bytes 9175040 | tf_op jit(solution)/shard_map/all_to_all | solution.py:43
  133.6 6.8 %convolution_convert_fusion.6 = bf16[640,512]{1,0:T(8,128)(2,1)} fusion(bf16[640,3584]{1,0:T(8,128)(2,1)} %bitcast.9, bf16[512,3584]{1,0:T(8,128)(2,1)} %all-gather.3.cloned.1.call-done), kind=kOutput, calls=%fused_computation.35 | convolution fusion | flops 2349137920 | bytes 8912896 | tf_op jit(solution)/shard_map/dot_general | solution.py:13
  140.4 8.5 %all-gather.5.cloned.1.call-done = bf16[3584,512]{1,0:T(8,128)(2,1)} async-done(((bf16[3584,256]{1,0:T(8,128)(2,1)}), bf16[3584,512]{1,0:T(8,128)(2,1)}) %all-gather.5.cloned.1.call-update) | async-done | bytes 3670032 | tf_op jit(solution)/shard_map/all_gather | solution.py:49
  148.9 84.9 %all-to-all-done.1 = bf16[4,160,3584]{2,1,0:T(8,128)(2,1)} async-done(((bf16[4,160,3584]{2,1,0:T(8,128)(2,1)}), bf16[4,160,3584]{2,1,0:T(8,128)(2,1)}, u32[]{:S(2)}, u32[]{:S(2)}) %all-to-all-start.1) | async-done | bytes 4587552 | tf_op jit(solution)/shard_map/all_to_all | solution.py:43
  233.8 6.8 %convolution_convert_fusion.5 = bf16[640,512]{1,0:T(8,128)(2,1)} fusion(bf16[640,3584]{1,0:T(8,128)(2,1)} %bitcast.12, bf16[3584,512]{1,0:T(8,128)(2,1)} %all-gather.5.cloned.1.call-done), kind=kOutput, calls=%fused_computation.34 | convolution fusion | flops 2349137920 | bytes 8912896 | tf_op jit(solution)/shard_map/dot_general | solution.py:52
  240.7 45.2 %all-reduce.3.cloned.1.call-done = (bf16[640,512]{1,0:T(8,128)(2,1)}, bf16[640,512]{1,0:T(8,128)(2,1)}) async-done(((bf16[640,512]{1,0:T(8,128)(2,1)}, bf16[640,512]{1,0:T(8,128)(2,1)}), (bf16[640,512]{1,0:T(8,128)(2,1)}, bf16[640,512]{1,0:T(8,128)(2,1)})) %all-reduce.3.cloned.1.call-update) | async-done | bytes 1310736 | tf_op jit(solution)/shard_map/psum | solution.py:55
  285.9 7.6 %convolution_convert_fusion.2 = bf16[3584,512]{1,0:T(8,128)(2,1)} fusion(bf16[640,3584]{1,0:T(8,128)(2,1)} %bitcast.12, bf16[640,512]{1,0:T(8,128)(2,1)} %get-tuple-element.7, bf16[640,512]{1,0:T(8,128)(2,1)} %get-tuple-element.8), kind=kOutput, calls=%fused_computation.8 | convolution fusion | flops 2354249728 | bytes 9568256 | tf_op jit(solution)/shard_map/dot_general | solution.py:13
  294.8 7.0 %convolution_convert_fusion = bf16[640,3584]{1,0:T(8,128)(2,1)} fusion(bf16[3584,512]{1,0:T(8,128)(2,1)} %all-gather.5.cloned.1.call-done, bf16[640,512]{1,0:T(8,128)(2,1)S(1)} %copy-done.3, bf16[640,512]{1,0:T(8,128)(2,1)S(1)} %copy-done.4), kind=kOutput, calls=%fused_computation.6 | convolution fusion | flops 2354708480 | bytes 9568256 | tf_op jit(solution)/shard_map/dot_general | solution.py:13
  301.8 5.0 %all-to-all-start.2 = ((bf16[4,160,3584]{2,1,0:T(8,128)(2,1)}), bf16[4,160,3584]{2,1,0:T(8,128)(2,1)}, u32[]{:S(2)}, u32[]{:S(2)}) async-start(bf16[4,160,3584]{2,1,0:T(8,128)(2,1)} %bitcast.49), calls=%async_computation.2 | async-start | bytes 9175040 | tf_op jit(solution)/shard_map/all_to_all | solution.py:73
  307.0 6.9 %convolution_convert_fusion.1 = bf16[512,3584]{1,0:T(8,128)(2,1)} fusion(bf16[640,3584]{1,0:T(8,128)(2,1)} %bitcast.9, bf16[640,512]{1,0:T(8,128)(2,1)S(1)} %copy-done.3), kind=kOutput, calls=%fused_computation.7 | convolution fusion | flops 2352611328 | bytes 8912896 | tf_op jit(solution)/shard_map/dot_general | solution.py:13
  314.0 94.9 %all-to-all-done.2 = bf16[4,160,3584]{2,1,0:T(8,128)(2,1)} async-done(((bf16[4,160,3584]{2,1,0:T(8,128)(2,1)}), bf16[4,160,3584]{2,1,0:T(8,128)(2,1)}, u32[]{:S(2)}, u32[]{:S(2)}) %all-to-all-start.2) | async-done | bytes 4587552 | tf_op jit(solution)/shard_map/all_to_all | solution.py:73
  408.9 3.5 convert.1
  412.5 2.7 fusion
  415.1 7.5 %gather_fusion = f32[256,3584]{1,0:T(8,128)} fusion(f32[320,3584]{1,0:T(8,128)} %bitcast.44, s32[1024]{0:T(1024)S(1)} %pad_clamp_fusion), kind=kCustom, calls=%fused_computation | custom fusion | bytes 7341056 | tf_op jit(solution)/shard_map/jit(_take)/gather | solution.py:82
  422.6 3.4 fusion.12
  426.0 4.9 %psum.38 = f32[256]{0:T(256)S(1)} all-reduce(f32[256]{0:T(256)S(1)} %get-tuple-element.6), channel_id=1, replica_groups=mesh['parts'=2,'expert'=4,'dp'=2,'tensor'=2] {'dp'}, use_global_device_ids=true, to_apply=%region_8.9 | all-reduce | flops 256 | bytes 2048 | tf_op jit(solution)/shard_map/psum | solution.py:86
  430.9 26.5 %psum.39 = f32[3584]{0:T(1024)} all-reduce(f32[3584]{0:T(1024)S(1)} %get-tuple-element.5), channel_id=1, replica_groups=mesh['parts'=2,'expert'=4,'dp'=2,'tensor'=2] {'expert','tensor'}, use_global_device_ids=true, to_apply=%region_12.13 | all-reduce | flops 3584 | bytes 28672 | tf_op jit(solution)/shard_map/psum | solution.py:84
  457.4 5.6 %fusion.3 = bf16[256,3584]{1,0:T(8,128)(2,1)} fusion(bf16[256,3584]{1,0:T(8,128)(2,1)} %param.8, bf16[256,3584]{1,0:T(8,128)(2,1)S(1)} %copy-done, f32[256,3584]{1,0:T(8,128)} %gather_fusion, f32[256]{0:T(256)S(1)} %psum.38, f32[256]{0:T(256)S(1)} %bitcast.57, f32[3584]{0:T(1024)S(1)} %copy-done.1, f32[256]{0:T(256)S(1)} %bitcast.54, ...), kind=kLoop, calls=%fused_computation.18 | loop fusion | flops 10092544 | bytes 9192704 | tf_op jit(solution)/shard_map/convert_element_type | solution.py:93
  (34 shorter events, 9.1 us)
Async XLA Ops:
  15.3 7.2 %copy-start = (bf16[256,3584]{1,0:T(8,128)(2,1)S(1)}, bf16[256,3584]{1,0:T(8,128)(2,1)}, u32[]{:S(2)}) copy-start(bf16[256,3584]{1,0:T(8,128)(2,1)} %param.7) | copy-start | bytes 5505028
  15.3 108.4 %all-to-all-start = ((bf16[4,160,3584]{2,1,0:T(8,128)(2,1)}), bf16[4,160,3584]{2,1,0:T(8,128)(2,1)}, u32[]{:S(2)}, u32[]{:S(2)}) async-start(bf16[4,160,3584]{2,1,0:T(8,128)(2,1)} %bitcast.46), calls=%async_computation | async-start | bytes 9175040 | tf_op jit(solution)/shard_map/all_to_all | solution.py:44
  21.7 6.1 %copy-start.1 = (f32[3584]{0:T(1024)S(1)}, f32[3584]{0:T(1024)}, u32[]{:S(2)}) copy-start(f32[3584]{0:T(1024)} %param.9) | copy-start | bytes 43012
  21.7 111.9 %all-gather.3.cloned.1.call-start = ((), (), s32[]{:S(2)}) async-start(), calls=%async_computation.5 | async-start | bytes 5505024 | tf_op jit(solution)/shard_map/all_gather | solution.py:50
  127.8 106.0 %all-to-all-start.1 = ((bf16[4,160,3584]{2,1,0:T(8,128)(2,1)}), bf16[4,160,3584]{2,1,0:T(8,128)(2,1)}, u32[]{:S(2)}, u32[]{:S(2)}) async-start(bf16[4,160,3584]{2,1,0:T(8,128)(2,1)} %bitcast.45), calls=%async_computation.1 | async-start | bytes 9175040 | tf_op jit(solution)/shard_map/all_to_all | solution.py:43
  132.8 16.2 %all-gather.5.cloned.1.call-start = ((), (), s32[]{:S(2)}) async-start(), calls=%async_computation.6 | async-start | bytes 5505024 | tf_op jit(solution)/shard_map/all_gather | solution.py:49
  133.5 152.4 %all-reduce.3.cloned.1.call-start = ((), (), s32[]{:S(2)}) async-start(), calls=%async_computation.9 | async-start | bytes 2621440 | tf_op jit(solution)/shard_map/psum | solution.py:55
  240.6 222.3 %reduce-scatter.3.cloned.1.call-start = ((), (), s32[]{:S(2)}) async-start(), calls=%async_computation.7 | async-start | bytes 5505024 | tf_op jit(solution)/shard_map/reduce_scatter | solution.py:66
  293.6 1.1 copy-start.3
  293.6 1.3 copy-start.4
  301.8 107.1 %all-to-all-start.2 = ((bf16[4,160,3584]{2,1,0:T(8,128)(2,1)}), bf16[4,160,3584]{2,1,0:T(8,128)(2,1)}, u32[]{:S(2)}, u32[]{:S(2)}) async-start(bf16[4,160,3584]{2,1,0:T(8,128)(2,1)} %bitcast.49), calls=%async_computation.2 | async-start | bytes 9175040 | tf_op jit(solution)/shard_map/all_to_all | solution.py:73
  306.8 156.2 %reduce-scatter.5.cloned.1.call-start = ((), (), s32[]{:S(2)}) async-start(), calls=%async_computation.8 | async-start | bytes 5505024 | tf_op jit(solution)/shard_map/reduce_scatter | solution.py:63
  430.9 32.1 %copy-start.2 = (f32[256]{0:T(256)}, f32[256]{0:T(256)S(1)}, u32[]{:S(2)}) copy-start(f32[256]{0:T(256)S(1)} %psum.38) | copy-start | bytes 3076
Sparse Core Ops, SparseCore 0:
  24.1 14.3 all-gather.2
  135.1 13.7 all-gather.4
  240.8 45.1 all-reduce.2
  293.7 11.5 reduce-scatter.2
  314.1 12.3 reduce-scatter.4
where the time goes:
time: 470 us
  waiting for transfers between devices  328 us (70%)
  matrix products  39.9 us (8%)
  blocking collectives  36.4 us (8%)
  other arithmetic  18.6 us (4%)
  starting transfers between devices  16.7 us (4%)
  local copies, waits for them, and re-layouts  15.6 us (3%)
  between operations  13.8 us (3%)
    all_to_all x1, waiting for transfers between devices, local(): lax.all_to_all(row_grad.reshape(n_expert, capacity, piece), 'expert', spl...  94.9 us
    all_to_all x1, waiting for transfers between devices, local(): lax.all_to_all(outward(packed_d), 'expert', split_axis=0, concat_axis=0,...  93.5 us
    all_to_all x1, waiting for transfers between devices, local(): lax.all_to_all(outward(packed_x), 'expert', split_axis=0, concat_axis=0,...  84.9 us
    psum x1, waiting for transfers between devices, local(): lax.psum(up_part.astype(jnp.bfloat16), 'dp').astype(jnp.float32)  45.2 us
    dot_general x6, matrix products, contract(): lax.dot_general(left, right, (((left_dim,), (right_dim,)), ((), ())), pre...  33.1 us
    psum x1, blocking collectives, local(): gain_grad = lax.psum(gain_terms, ('expert', 'tensor'))  26.5 us
  transfers between devices with their start and end apart: 8, of which 5 were waited for; matrix products, arithmetic and copies ran while one was open for 11% of the time, Pallas kernels for 0%

commit v1 on v0

--- a/solution.py
+++ b/solution.py
@@ -93,7 +93,134 @@
     return (token_grad.astype(jnp.bfloat16), up_grad, down_grad, gain_grad, inner[:, 0])
 
 
+def after(value, *earlier):
+    return lax.optimization_barrier((value,) + earlier)[0]
+
+
+def swap(value, axis):
+    return lax.ppermute(value, axis, ((0, 1), (1, 0)))
+
+
+def local_line(
+    tokens, cotangent, norm_gain, expert_ids, combine_weight, up_weight, down_weight
+):
+    count, piece = tokens.shape
+    width = piece * 2
+    capacity = count * 5 // 8
+    inward, middle, outward = ((0, 1), (3, 2)), ((1, 2), (2, 1)), ((1, 0), (2, 3))
+    place = lax.axis_index("expert")
+    mine = place // 2
+    is_inner = (place == 1) | (place == 2)
+    part = lax.axis_index("parts")
+
+    tokens_in = lax.ppermute(tokens, "expert", inward)
+    half_up = lax.dynamic_slice_in_dim(up_weight, part * (piece // 2), piece // 2, 0)
+    rows_down = down_weight.shape[0] // 2
+    half_down = lax.dynamic_slice_in_dim(down_weight, part * rows_down, rows_down, 0)
+    half_up = lax.ppermute(after(half_up, tokens_in), "expert", inward)
+    cotangent_in = lax.ppermute(after(cotangent, half_up), "expert", inward)
+    half_down = lax.ppermute(after(half_down, cotangent_in), "expert", inward)
+
+    token_f = tokens.astype(jnp.float32)
+    squares = lax.psum(jnp.sum(token_f * token_f, axis=1), "dp")
+    scale = lax.rsqrt(squares / width + 1e-06)
+    target = expert_ids[:, 0]
+    small = jnp.stack([scale, combine_weight, target.astype(jnp.float32)])
+    small_in = lax.ppermute(small, "expert", inward)
+
+    def pack(block, cot_block, facts):
+        scale_b, gate_b = facts[0][:, None], facts[1][:, None]
+        target_b = facts[2].astype(jnp.int32)
+        normed = (block.astype(jnp.float32) * scale_b * norm_gain[None, :]).astype(jnp.bfloat16)
+        scaled = (gate_b * cot_block.astype(jnp.float32)).astype(jnp.bfloat16)
+
+        def places(expert):
+            hit = target_b == expert
+            slot = jnp.where(hit, jnp.cumsum(hit.astype(jnp.int32)) - 1, -1)
+            return (slot[:, None] == jnp.arange(capacity, dtype=jnp.int32)[None, :]).astype(
+                jnp.bfloat16
+            )
+
+        keep, send = places(mine), places(1 - mine)
+
+        def picked(where, rows):
+            return contract(where, rows, 0, 0).astype(jnp.bfloat16)
+
+        return keep, send, normed, scaled, picked
+
+    keep_a, send_a, normed_a, scaled_a, picked = pack(tokens, cotangent, small)
+    keep_b, send_b, normed_b, scaled_b, picked = pack(tokens_in, cotangent_in, small_in)
+    far_xa = lax.ppermute(picked(send_a, normed_a), "expert", middle)
+    far_da = lax.ppermute(picked(send_a, scaled_a), "expert", middle)
+    far_xb = lax.ppermute(picked(send_b, normed_b), "expert", middle)
+    far_db = lax.ppermute(picked(send_b, scaled_b), "expert", middle)
+
+    def joined(half, own, axis):
+        other = swap(half, "parts")
+        first = jnp.where(part == 0, half, other)
+        second = jnp.where(part == 0, other, half)
+        outer = jnp.concatenate([first, second], axis=0)
+        both = jnp.concatenate([own, outer], axis=axis)
+        return lax.all_gather(both, "tensor", axis=axis, tiled=True)
+
+    full_up = joined(half_up, up_weight, 1)
+    full_down = joined(half_down, down_weight, 0)
+    rows_x = jnp.concatenate([far_xa, far_xb, picked(keep_a, normed_a), picked(keep_b, normed_b)])
+    rows_d = jnp.concatenate([far_da, far_db, picked(keep_a, scaled_a), picked(keep_b, scaled_b)])
+
+    def over_dp(value):
+        rounded = value.astype(jnp.bfloat16)
+        return rounded.astype(jnp.float32) + swap(rounded, "dp").astype(jnp.float32)
+
+    pre = over_dp(contract(rows_x, full_up, 1, 0))
+    back = over_dp(contract(rows_d, full_down, 1, 1))
+    act = jax.nn.silu(pre).astype(jnp.bfloat16)
+    dpre = (back * slope(pre)).astype(jnp.bfloat16)
+    span = 2 * capacity
+    far_grad = contract(dpre[:span], full_up, 1, 1).astype(jnp.bfloat16)
+    back_b = lax.ppermute(far_grad[capacity:], "expert", middle)
+    back_a = lax.ppermute(far_grad[:capacity], "expert", middle)
+    near_grad = contract(dpre[span:], full_up, 1, 1).astype(jnp.bfloat16)
+
+    def restored(keep, near, send, far):
+        return (contract(keep, near, 1, 0) + contract(send, far, 1, 0)).astype(jnp.bfloat16)
+
+    grad_b = restored(keep_b, near_grad[capacity:], send_b, back_b)
+    grad_in = lax.ppermute(grad_b, "expert", outward)
+    grad_a = restored(keep_a, near_grad[:capacity], send_a, back_a)
+
+    side = lax.axis_index("tensor")
+
+    def shared(terms, axis):
+        size = terms.shape[axis] // 2
+        own = lax.dynamic_slice_in_dim(terms, side * size, size, axis)
+        other = lax.dynamic_slice_in_dim(terms, (1 - side) * size, size, axis)
+        total = own + swap(other.astype(jnp.bfloat16), "tensor").astype(jnp.float32)
+        total = total.astype(jnp.bfloat16)
+        inner_half, outer_half = jnp.split(total, 2, axis=axis)
+        arrived = lax.ppermute(outer_half, "expert", outward)
+        return jnp.where(is_inner, inner_half, arrived)
+
+    down_grad = shared(contract(act, rows_d, 0, 0), 0)
+    up_grad = shared(contract(rows_x, dpre, 0, 0), 1)
+
+    normed_grad = jnp.where(is_inner, grad_a, grad_in).astype(jnp.float32)
+    scale = scale[:, None]
+    gain_grad = lax.psum(jnp.sum(normed_grad * token_f * scale, axis=0), ("expert", "tensor"))
+    inner_part = jnp.sum(token_f * norm_gain[None, :] * normed_grad, axis=1)
+    inner = lax.psum(inner_part, "dp")
+    cubed = scale * scale * scale
+    token_grad = (
+        cotangent.astype(jnp.float32)
+        + scale * norm_gain[None, :] * normed_grad
+        - token_f * cubed * inner[:, None] / width
+    )
+    return (token_grad.astype(jnp.bfloat16), up_grad, down_grad, gain_grad, inner)
+
+
 def solution(mesh):
+    sizes = tuple(mesh.shape[name] for name in ("parts", "expert", "dp", "tensor"))
+    body = local_line if sizes == (2, 4, 2, 2) else local
     in_specs = (
         P(("parts", "expert", "tensor"), "dp"),
         P(("parts", "expert", "tensor"), "dp"),
@@ -110,4 +237,4 @@
         P(("parts", "dp")),
         P(("parts", "expert", "tensor")),
     )
-    return jax.shard_map(local, mesh=mesh, in_specs=in_specs, out_specs=out_specs, check_vma=False)
+    return jax.shard_map(body, mesh=mesh, in_specs=in_specs, out_specs=out_specs, check_vma=False)

time: 470 us -> 547 us (1.16); the launches traced: 470 us -> 538 us
  waiting for transfers between devices: 328 us -> 284 us
  matrix products: 39.9 us -> 75 us
  starting transfers between devices: 16.7 us -> 44.2 us
  other arithmetic: 18.6 us -> 40.9 us
  blocking collectives: 36.4 us -> 57.8 us
    ppermute x0 -> x20, waiting for transfers between devices: none -> 284 us  [the longest x2 78.1 us: shared(): arrived = lax.ppermute(outer_half, 'expert', outward)]
    all_to_all x3 -> x0, waiting for transfers between devices: 273 us -> none  [the longest x1 94.9 us: local(): lax.all_to_all(row_grad.reshape(n_expert, capacity, piece), 'expert', spl...]
    psum x1 -> x0, waiting for transfers between devices: 45.2 us -> none  [local(): lax.psum(up_part.astype(jnp.bfloat16), 'dp').astype(jnp.float32)]
    ppermute x0 -> x20, starting transfers between devices: none -> 44.1 us  [the longest x1 6.18 us: local_line(): tokens_in = lax.ppermute(tokens, 'expert', inward)]
    dot_general x6 -> x18, matrix products: 33.1 us -> 75 us  [contract(): lax.dot_general(left, right, (((left_dim,), (right_dim,)), ((), ())), pre...]
    psum x3, blocking collectives: 36.4 us -> 57.8 us  [the longest x1 48 us: local_line(): lax.psum(jnp.sum(normed_grad * token_f * scale, axis=0), ('expert', 'tens...]
    all_to_all x3 -> x0, starting transfers between devices: 16.4 us -> none  [the longest x1 6.45 us: local(): lax.all_to_all(outward(packed_d), 'expert', split_axis=0, concat_axis=0,...]
    concatenate x0 -> x2, other arithmetic: none -> 12.5 us  [joined(): both = jnp.concatenate([own, outer], axis=axis)]
  transfers between devices with their start and end apart: 8 -> 22, of which waited for: 5 -> 10; matrix products, arithmetic and copies ran while one was open for 11% -> 21% of each run, Pallas kernels for 0% -> 0%
where the time goes in v1:
time: 547 us; the launch traced here: 538 us
  waiting for transfers between devices  284 us (52%)
  matrix products  75 us (14%)
  blocking collectives  57.8 us (11%)
  starting transfers between devices  44.2 us (8%)
  other arithmetic  40.9 us (7%)
  local copies, waits for them, and re-layouts  21 us (4%)
  between operations  14.8 us (3%)
    ppermute x2, waiting for transfers between devices, shared(): arrived = lax.ppermute(outer_half, 'expert', outward)  78.1 us
    dot_general x18, matrix products, contract(): lax.dot_general(left, right, (((left_dim,), (right_dim,)), ((), ())), pre...  75 us
    ppermute x6, waiting for transfers between devices, swap(): return lax.ppermute(value, axis, ((0, 1), (1, 0)))  64.1 us
    psum x1, blocking collectives, local_line(): lax.psum(jnp.sum(normed_grad * token_f * scale, axis=0), ('expert', 'tens...  48 us
    ppermute x1, waiting for transfers between devices, local_line(): tokens_in = lax.ppermute(tokens, 'expert', inward)  36.9 us
    ppermute x1, waiting for transfers between devices, local_line(): grad_in = lax.ppermute(grad_b, 'expert', outward)  36.4 us
    ppermute x1, waiting for transfers between devices, local_line(): cotangent_in = lax.ppermute(after(cotangent, half_up), 'expert', inward)  33.8 us
    ppermute x1, waiting for transfers between devices, local_line(): half_up = lax.ppermute(after(half_up, tokens_in), 'expert', inward)  18.7 us
  transfers between devices with their start and end apart: 22, of which 10 were waited for; matrix products, arithmetic and copies ran while one was open for 21% of the time, Pallas kernels for 0%

profile of v1, /device:TPU:0, one launch (start us, length us, event | category | flops | bytes accessed | tf_op | source)
XLA Modules:
  0.0 537.6 jit_solution(186196391655998980)
XLA Ops:
  7.2 6.2 %collective-permute-start.2 = (bf16[256,3584]{1,0:T(8,128)(2,1)}, bf16[256,3584]{1,0:T(8,128)(2,1)}, u32[]{:S(2)}, u32[]{:S(2)}) collective-permute-start(bf16[256,3584]{1,0:T(8,128)(2,1)} %param.7), channel_id=1, source_target_pairs={{0,4},{12,8},{1,5},{13,9},{2,6},{14,10},{3,7},{15,11},{16,20},{28,... | collective-permute-start | bytes 5505032 | tf_op jit(solution)/shard_map/ppermute | solution.py:116
  14.8 36.9 %collective-permute-done.2 = bf16[256,3584]{1,0:T(8,128)(2,1)} collective-permute-done((bf16[256,3584]{1,0:T(8,128)(2,1)}, bf16[256,3584]{1,0:T(8,128)(2,1)}, u32[]{:S(2)}, u32[]{:S(2)}) %collective-permute-start.2) | collective-permute-done | bytes 1835040 | tf_op jit(solution)/shard_map/ppermute | solution.py:116
  56.2 18.7 %collective-permute-done.3 = bf16[1792,256]{1,0:T(8,128)(2,1)S(1)} collective-permute-done((bf16[1792,256]{1,0:T(8,128)(2,1)S(1)}, bf16[1792,256]{1,0:T(8,128)(2,1)S(1)}, u32[]{:S(2)}, u32[]{:S(2)}) %collective-permute-start.3) | collective-permute-done | bytes 917536 | tf_op jit(solution)/shard_map/ppermute | solution.py:120
  76.3 18.9 %collective-permute-done.11 = bf16[1792,256]{1,0:T(8,128)(2,1)} collective-permute-done((bf16[1792,256]{1,0:T(8,128)(2,1)S(1)}, bf16[1792,256]{1,0:T(8,128)(2,1)}, u32[]{:S(2)}, u32[]{:S(2)}) %collective-permute-start.11) | collective-permute-done | bytes 917536 | tf_op jit(solution)/shard_map/ppermute | solution.py:101
  96.5 10.5 %maximum_maximum_fusion = bf16[3584,512]{1,0:T(8,128)(2,1)} fusion(bf16[1792,256]{1,0:T(8,128)(2,1)S(1)} %get-tuple-element.20, bf16[1792,256]{1,0:T(8,128)(2,1)S(1)} %get-tuple-element.19, bf16[3584,256]{1,0:T(8,128)(2,1)S(1)} %copy-done.7), kind=kLoop, calls=%fused_computation.42 | loop fusion | flops 11010048 | bytes 7340032 | tf_op jit(solution)/shard_map/concatenate | solution.py:163
  108.5 5.6 %collective-permute-start.4 = (bf16[256,3584]{1,0:T(8,128)(2,1)S(1)}, bf16[256,3584]{1,0:T(8,128)(2,1)}, u32[]{:S(2)}, u32[]{:S(2)}) collective-permute-start(bf16[256,3584]{1,0:T(8,128)(2,1)S(1)} %copy-done), channel_id=1, source_target_pairs={{0,4},{12,8},{1,5},{13,9},{2,6},{14,10},{3,7},{15,11},{16,20},{28,... | collective-permute-start | bytes 5505032 | tf_op jit(solution)/shard_map/ppermute | solution.py:121
  115.6 33.8 %collective-permute-done.4 = bf16[256,3584]{1,0:T(8,128)(2,1)} collective-permute-done((bf16[256,3584]{1,0:T(8,128)(2,1)S(1)}, bf16[256,3584]{1,0:T(8,128)(2,1)}, u32[]{:S(2)}, u32[]{:S(2)}) %collective-permute-start.4) | collective-permute-done | bytes 1835040 | tf_op jit(solution)/shard_map/ppermute | solution.py:121
  154.0 15.9 %collective-permute-done.6 = bf16[128,3584]{1,0:T(8,128)(2,1)S(1)} collective-permute-done((bf16[128,3584]{1,0:T(8,128)(2,1)S(1)}, bf16[128,3584]{1,0:T(8,128)(2,1)S(1)}, u32[]{:S(2)}, u32[]{:S(2)}) %collective-permute-start.6) | collective-permute-done | bytes 917536 | tf_op jit(solution)/shard_map/ppermute | solution.py:122
  171.4 16.0 %collective-permute-done.7 = bf16[128,3584]{1,0:T(8,128)(2,1)S(1)} collective-permute-done((bf16[128,3584]{1,0:T(8,128)(2,1)S(1)}, bf16[128,3584]{1,0:T(8,128)(2,1)S(1)}, u32[]{:S(2)}, u32[]{:S(2)}) %collective-permute-start.7) | collective-permute-done | bytes 917536 | tf_op jit(solution)/shard_map/ppermute | solution.py:101
  193.1 4.9 psum.21
  230.0 9.4 %convolution_convert_fusion.10 = bf16[640,1024]{1,0:T(8,128)(2,1)S(1)} fusion(bf16[3584,1024]{1,0:T(8,128)(2,1)} %all-gather.5.cloned.1.call-done, bf16[160,3584]{1,0:T(8,128)(2,1)} %convolution_convert_fusion.2, bf16[160,3584]{1,0:T(8,128)(2,1)} %convolution_convert_fusion.3, bf16[160,3584]{1,0:T(8,128)(2,1)} %collective-permute-done.10, ...), kind=kOutput, calls=%fused_computation.51 | convolution fusion | flops 4716625920 | bytes 13238272 | tf_op jit(solution)/shard_map/dot_general | solution.py:13
  241.0 9.5 %convolution_convert_fusion.11 = bf16[640,1024]{1,0:T(8,128)(2,1)S(1)} fusion(bf16[1024,3584]{1,0:T(8,128)(2,1)} %all-gather.3.cloned.1.call-done, bf16[160,3584]{1,0:T(8,128)(2,1)} %convolution_convert_fusion.6, bf16[160,3584]{1,0:T(8,128)(2,1)} %convolution_convert_fusion.7, bf16[160,3584]{1,0:T(8,128)(2,1)} %collective-permute-done.5, ...), kind=kOutput, calls=%fused_computation.52 | convolution fusion | flops 4716625920 | bytes 13238272 | tf_op jit(solution)/shard_map/dot_general | solution.py:13
  251.1 20.2 %collective-permute-done.12 = bf16[640,1024]{1,0:T(8,128)(2,1)} collective-permute-done((bf16[640,1024]{1,0:T(8,128)(2,1)S(1)}, bf16[640,1024]{1,0:T(8,128)(2,1)}, u32[]{:S(2)}, u32[]{:S(2)}) %collective-permute-start.12) | collective-permute-done | bytes 1310752 | tf_op jit(solution)/shard_map/ppermute | solution.py:101
  271.3 8.3 %fusion.14 = f32[1024,3584]{1,0:T(8,128)S(1)} fusion(bf16[640,1024]{1,0:T(8,128)(2,1)} %collective-permute-done.12, bf16[640,1024]{1,0:T(8,128)(2,1)S(1)} %convolution_convert_fusion.10, bf16[160,3584]{1,0:T(8,128)(2,1)S(1)} %copy-done.14, bf16[160,3584]{1,0:T(8,128)(2,1)S(1)} %copy-done.13, bf16[160,3584]{1,0:T(8,128)(2,1)} %collective-permute-done.5, ...), kind=kOutput, calls=%fused_computation.53 | convolution fusion | flops 4721213440 | bytes 21889024 | tf_op jit(solution)/shard_map/dot_general | solution.py:13
  282.1 9.0 %collective-permute-done.8 = bf16[640,1024]{1,0:T(8,128)(2,1)S(1)} collective-permute-done((bf16[640,1024]{1,0:T(8,128)(2,1)S(1)}, bf16[640,1024]{1,0:T(8,128)(2,1)S(1)}, u32[]{:S(2)}, u32[]{:S(2)}) %collective-permute-start.8) | collective-permute-done | bytes 1310752 | tf_op jit(solution)/shard_map/ppermute | solution.py:101
  294.9 7.6 %fusion.20 = f32[3584,1024]{1,0:T(8,128)S(1)} fusion(bf16[640,1024]{1,0:T(8,128)(2,1)S(1)} %multiply_convert_fusion.3, bf16[160,3584]{1,0:T(8,128)(2,1)} %convolution_convert_fusion.2, bf16[160,3584]{1,0:T(8,128)(2,1)} %convolution_convert_fusion.3, bf16[160,3584]{1,0:T(8,128)(2,1)} %collective-permute-done.10, bf16[160,3584]{1,0:T(8,128)(2,1)S(1)} %copy-done.20), kind=kOutput, calls=%fused_computation.63 | convolution fusion | flops 4715970560 | bytes 20578304 | tf_op jit(solution)/shard_map/dot_general | solution.py:13
  302.6 5.2 copy-done.3
  309.1 5.7 %convolution_convert_fusion = bf16[320,3584]{1,0:T(8,128)(2,1)S(1)} fusion(bf16[3584,1024]{1,0:T(8,128)(2,1)} %all-gather.5.cloned.1.call-done, bf16[640,1024]{1,0:T(8,128)(2,1)S(1)} %copy-done.11), kind=kOutput, calls=%fused_computation.13 | convolution fusion | flops 2349957120 | bytes 10289152 | tf_op jit(solution)/shard_map/dot_general | solution.py:13
  319.8 5.7 %convolution_convert_fusion.1 = bf16[320,3584]{1,0:T(8,128)(2,1)S(1)} fusion(bf16[3584,1024]{1,0:T(8,128)(2,1)} %all-gather.5.cloned.1.call-done, bf16[640,1024]{1,0:T(8,128)(2,1)S(1)} %copy-done.12), kind=kOutput, calls=%fused_computation.14 | convolution fusion | flops 2349957120 | bytes 10289152 | tf_op jit(solution)/shard_map/dot_general | solution.py:13
  326.2 5.3 add_convert_fusion
  347.3 78.1 %collective-permute-done.19 = bf16[256,3584]{1,0:T(8,128)(2,1)} collective-permute-done((bf16[256,3584]{1,0:T(8,128)(2,1)}, bf16[256,3584]{1,0:T(8,128)(2,1)}, u32[]{:S(2)}, u32[]{:S(2)}) %collective-permute-start.19) | collective-permute-done | bytes 1835040 | tf_op jit(solution)/shard_map/ppermute | solution.py:201
  428.3 36.4 %collective-permute-done.15 = bf16[256,3584]{1,0:T(8,128)(2,1)} collective-permute-done((bf16[256,3584]{1,0:T(8,128)(2,1)S(1)}, bf16[256,3584]{1,0:T(8,128)(2,1)}, u32[]{:S(2)}, u32[]{:S(2)}) %collective-permute-start.15) | collective-permute-done | bytes 1835040 | tf_op jit(solution)/shard_map/ppermute | solution.py:189
  474.4 48.0 %psum.23 = f32[3584]{0:T(1024)} all-reduce(f32[3584]{0:T(1024)S(1)} %get-tuple-element.11), channel_id=1, replica_groups=mesh['parts'=2,'expert'=4,'dp'=2,'tensor'=2] {'expert','tensor'}, use_global_device_ids=true, to_apply=%region_13.14 | all-reduce | flops 3584 | bytes 28672 | tf_op jit(solution)/shard_map/psum | solution.py:209
  522.3 5.1 fusion.5
  (128 shorter events, 102.2 us)
Async XLA Ops:
  7.2 222.9 %all-gather.5.cloned.1.call-start = ((), (), s32[]{:S(2)}) async-start(), calls=%async_computation.1 | async-start | bytes 11010048 | tf_op jit(solution)/shard_map/all_gather | solution.py:164
  7.2 44.5 %collective-permute-start.2 = (bf16[256,3584]{1,0:T(8,128)(2,1)}, bf16[256,3584]{1,0:T(8,128)(2,1)}, u32[]{:S(2)}, u32[]{:S(2)}) collective-permute-start(bf16[256,3584]{1,0:T(8,128)(2,1)} %param.7), channel_id=1, source_target_pairs={{0,4},{12,8},{1,5},{13,9},{2,6},{14,10},{3,7},{15,11},{16,20},{28,... | collective-permute-start | bytes 5505032 | tf_op jit(solution)/shard_map/ppermute | solution.py:116
  51.7 23.1 %collective-permute-start.3 = (bf16[1792,256]{1,0:T(8,128)(2,1)S(1)}, bf16[1792,256]{1,0:T(8,128)(2,1)S(1)}, u32[]{:S(2)}, u32[]{:S(2)}) collective-permute-start(bf16[1792,256]{1,0:T(8,128)(2,1)S(1)} %constant_dynamic-slice_fusion.1), channel_id=1, source_target_pairs={{0,4},{12,8},{1,5},{13,9},{2,6},{14,10},{3,7},{15,11},{16,20},{28,... | collective-permute-start | bytes 2752520 | tf_op jit(solution)/shard_map/ppermute | solution.py:120
  74.8 20.4 %collective-permute-start.11 = (bf16[1792,256]{1,0:T(8,128)(2,1)S(1)}, bf16[1792,256]{1,0:T(8,128)(2,1)}, u32[]{:S(2)}, u32[]{:S(2)}) collective-permute-start(bf16[1792,256]{1,0:T(8,128)(2,1)S(1)} %collective-permute-done.3), channel_id=1, source_target_pairs={{0,16},{16,0},{1,17},{17,1},{2,18},{18,2},{3,19},{19,3},{4,20},{20... | collective-permute-start | bytes 2752520 | tf_op jit(solution)/shard_map/ppermute | solution.py:101
  107.0 134.0 %all-gather.3.cloned.1.call-start = ((), (), s32[]{:S(2)}) async-start(), calls=%async_computation | async-start | bytes 11010048 | tf_op jit(solution)/shard_map/all_gather | solution.py:164
  108.5 40.9 %collective-permute-start.4 = (bf16[256,3584]{1,0:T(8,128)(2,1)S(1)}, bf16[256,3584]{1,0:T(8,128)(2,1)}, u32[]{:S(2)}, u32[]{:S(2)}) collective-permute-start(bf16[256,3584]{1,0:T(8,128)(2,1)S(1)} %copy-done), channel_id=1, source_target_pairs={{0,4},{12,8},{1,5},{13,9},{2,6},{14,10},{3,7},{15,11},{16,20},{28,... | collective-permute-start | bytes 5505032 | tf_op jit(solution)/shard_map/ppermute | solution.py:121
  149.4 20.4 %collective-permute-start.6 = (bf16[128,3584]{1,0:T(8,128)(2,1)S(1)}, bf16[128,3584]{1,0:T(8,128)(2,1)S(1)}, u32[]{:S(2)}, u32[]{:S(2)}) collective-permute-start(bf16[128,3584]{1,0:T(8,128)(2,1)S(1)} %constant_dynamic-slice_fusion), channel_id=1, source_target_pairs={{0,4},{12,8},{1,5},{13,9},{2,6},{14,10},{3,7},{15,11},{16,20},{28,... | collective-permute-start | bytes 2752520 | tf_op jit(solution)/shard_map/ppermute | solution.py:122
  169.9 17.5 %collective-permute-start.7 = (bf16[128,3584]{1,0:T(8,128)(2,1)S(1)}, bf16[128,3584]{1,0:T(8,128)(2,1)S(1)}, u32[]{:S(2)}, u32[]{:S(2)}) collective-permute-start(bf16[128,3584]{1,0:T(8,128)(2,1)S(1)} %collective-permute-done.6), channel_id=1, source_target_pairs={{0,16},{16,0},{1,17},{17,1},{2,18},{18,2},{3,19},{19,3},{4,20},{20... | collective-permute-start | bytes 2752520 | tf_op jit(solution)/shard_map/ppermute | solution.py:101
  198.3 14.0 %collective-permute-start.1 = (f32[3,256]{1,0:T(4,128)S(1)}, f32[3,256]{1,0:T(4,128)S(1)}, u32[]{:S(2)}, u32[]{:S(2)}) collective-permute-start(f32[3,256]{1,0:T(4,128)S(1)} %pad_maximum_fusion.7), channel_id=1, source_target_pairs={{0,4},{12,8},{1,5},{13,9},{2,6},{14,10},{3,7},{15,11},{16,20},{28,... | collective-permute-start | bytes 9224 | tf_op jit(solution)/shard_map/ppermute | solution.py:129
  204.5 36.4 %collective-permute-start = (bf16[160,3584]{1,0:T(8,128)(2,1)}, bf16[160,3584]{1,0:T(8,128)(2,1)}, u32[]{:S(2)}, u32[]{:S(2)}) collective-permute-start(bf16[160,3584]{1,0:T(8,128)(2,1)} %convolution_convert_fusion.9), channel_id=1, source_target_pairs={{4,8},{8,4},{5,9},{9,5},{6,10},{10,6},{7,11},{11,7},{20,24},{24,20... | collective-permute-start | bytes 3440648 | tf_op jit(solution)/shard_map/ppermute | solution.py:154
  208.1 20.9 %collective-permute-start.9 = (bf16[160,3584]{1,0:T(8,128)(2,1)}, bf16[160,3584]{1,0:T(8,128)(2,1)S(1)}, u32[]{:S(2)}, u32[]{:S(2)}) collective-permute-start(bf16[160,3584]{1,0:T(8,128)(2,1)} %convolution_convert_fusion.5), channel_id=1, source_target_pairs={{4,8},{8,4},{5,9},{9,5},{6,10},{10,6},{7,11},{11,7},{20,24},{24,20... | collective-permute-start | bytes 3440648 | tf_op jit(solution)/shard_map/ppermute | solution.py:153
  215.7 13.3 %collective-permute-start.10 = (bf16[160,3584]{1,0:T(8,128)(2,1)S(1)}, bf16[160,3584]{1,0:T(8,128)(2,1)}, u32[]{:S(2)}, u32[]{:S(2)}) collective-permute-start(bf16[160,3584]{1,0:T(8,128)(2,1)S(1)} %convolution_convert_fusion.4), channel_id=1, source_target_pairs={{4,8},{8,4},{5,9},{9,5},{6,10},{10,6},{7,11},{11,7},{20,24},{24,20... | collective-permute-start | bytes 3440648 | tf_op jit(solution)/shard_map/ppermute | solution.py:155
  224.0 16.9 %collective-permute-start.5 = (bf16[160,3584]{1,0:T(8,128)(2,1)}, bf16[160,3584]{1,0:T(8,128)(2,1)}, u32[]{:S(2)}, u32[]{:S(2)}) collective-permute-start(bf16[160,3584]{1,0:T(8,128)(2,1)} %convolution_convert_fusion.8), channel_id=1, source_target_pairs={{4,8},{8,4},{5,9},{9,5},{6,10},{10,6},{7,11},{11,7},{20,24},{24,20... | collective-permute-start | bytes 3440648 | tf_op jit(solution)/shard_map/ppermute | solution.py:156
  239.4 31.9 %collective-permute-start.12 = (bf16[640,1024]{1,0:T(8,128)(2,1)S(1)}, bf16[640,1024]{1,0:T(8,128)(2,1)}, u32[]{:S(2)}, u32[]{:S(2)}) collective-permute-start(bf16[640,1024]{1,0:T(8,128)(2,1)S(1)} %convolution_convert_fusion.10), channel_id=1, source_target_pairs={{0,2},{2,0},{1,3},{3,1},{4,6},{6,4},{5,7},{7,5},{8,10},{10,8},{9,1... | collective-permute-start | bytes 3932168 | tf_op jit(solution)/shard_map/ppermute | solution.py:101
  250.6 40.6 %collective-permute-start.8 = (bf16[640,1024]{1,0:T(8,128)(2,1)S(1)}, bf16[640,1024]{1,0:T(8,128)(2,1)S(1)}, u32[]{:S(2)}, u32[]{:S(2)}) collective-permute-start(bf16[640,1024]{1,0:T(8,128)(2,1)S(1)} %convolution_convert_fusion.11), channel_id=1, source_target_pairs={{0,2},{2,0},{1,3},{3,1},{4,6},{6,4},{5,7},{7,5},{8,10},{10,8},{9,1... | collective-permute-start | bytes 3932168 | tf_op jit(solution)/shard_map/ppermute | solution.py:101
  282.1 44.1 %collective-permute-start.18 = (bf16[512,3584]{1,0:T(8,128)(2,1)}, bf16[512,3584]{1,0:T(8,128)(2,1)}, u32[]{:S(2)}, u32[]{:S(2)}) collective-permute-start(bf16[512,3584]{1,0:T(8,128)(2,1)} %dynamic-slice_convert_fusion), channel_id=1, source_target_pairs={{0,1},{1,0},{2,3},{3,2},{4,5},{5,4},{6,7},{7,6},{8,9},{9,8},{10,11... | collective-permute-start | bytes 11010056 | tf_op jit(solution)/shard_map/ppermute | solution.py:101
  308.3 31.5 %collective-permute-start.16 = (bf16[3584,512]{1,0:T(8,128)(2,1)S(1)}, bf16[3584,512]{1,0:T(8,128)(2,1)S(1)}, u32[]{:S(2)}, u32[]{:S(2)}) collective-permute-start(bf16[3584,512]{1,0:T(8,128)(2,1)S(1)} %dynamic-slice_convert_fusion.1), channel_id=1, source_target_pairs={{0,1},{1,0},{2,3},{3,2},{4,5},{5,4},{6,7},{7,6},{8,9},{9,8},{10,11... | collective-permute-start | bytes 11010056 | tf_op jit(solution)/shard_map/ppermute | solution.py:101
  316.3 112.0 %collective-permute-start.13 = (bf16[160,3584]{1,0:T(8,128)(2,1)}, bf16[160,3584]{1,0:T(8,128)(2,1)}, u32[]{:S(2)}, u32[]{:S(2)}) collective-permute-start(bf16[160,3584]{1,0:T(8,128)(2,1)} %get-tuple-element.15), channel_id=1, source_target_pairs={{4,8},{8,4},{5,9},{9,5},{6,10},{10,6},{7,11},{11,7},{20,24},{24,20... | collective-permute-start | bytes 3440648 | tf_op jit(solution)/shard_map/ppermute | solution.py:182
  317.9 18.6 %collective-permute-start.14 = (bf16[160,3584]{1,0:T(8,128)(2,1)}, bf16[160,3584]{1,0:T(8,128)(2,1)}, u32[]{:S(2)}, u32[]{:S(2)}) collective-permute-start(bf16[160,3584]{1,0:T(8,128)(2,1)} %get-tuple-element.16), channel_id=1, source_target_pairs={{4,8},{8,4},{5,9},{9,5},{6,10},{10,6},{7,11},{11,7},{20,24},{24,20... | collective-permute-start | bytes 3440648 | tf_op jit(solution)/shard_map/ppermute | solution.py:181
  332.8 92.5 %collective-permute-start.19 = (bf16[256,3584]{1,0:T(8,128)(2,1)}, bf16[256,3584]{1,0:T(8,128)(2,1)}, u32[]{:S(2)}, u32[]{:S(2)}) collective-permute-start(bf16[256,3584]{1,0:T(8,128)(2,1)} %split.19), channel_id=1, source_target_pairs={{4,0},{8,12},{5,1},{9,13},{6,2},{10,14},{7,3},{11,15},{20,16},{24,... | collective-permute-start | bytes 5505032 | tf_op jit(solution)/shard_map/ppermute | solution.py:201
  338.5 126.1 %collective-permute-start.15 = (bf16[256,3584]{1,0:T(8,128)(2,1)S(1)}, bf16[256,3584]{1,0:T(8,128)(2,1)}, u32[]{:S(2)}, u32[]{:S(2)}) collective-permute-start(bf16[256,3584]{1,0:T(8,128)(2,1)S(1)} %fusion.1), channel_id=1, source_target_pairs={{4,0},{8,12},{5,1},{9,13},{6,2},{10,14},{7,3},{11,15},{20,16},{24,... | collective-permute-start | bytes 5505032 | tf_op jit(solution)/shard_map/ppermute | solution.py:189
  345.7 118.9 %copy-start.6 = (bf16[256,3584]{1,0:T(8,128)(2,1)S(1)}, bf16[256,3584]{1,0:T(8,128)(2,1)}, u32[]{:S(2)}) copy-start(bf16[256,3584]{1,0:T(8,128)(2,1)} %param.7) | copy-start | bytes 5505028
  345.7 118.9 %copy-start.9 = (f32[256,3584]{1,0:T(8,128)S(1)}, f32[256,3584]{1,0:T(8,128)}, u32[]{:S(2)}) copy-start(f32[256,3584]{1,0:T(8,128)} %fusion.18) | copy-start | bytes 11010052
  345.7 181.7 %collective-permute-start.17 = (bf16[3584,256]{1,0:T(8,128)(2,1)}, bf16[3584,256]{1,0:T(8,128)(2,1)}, u32[]{:S(2)}, u32[]{:S(2)}) collective-permute-start(bf16[3584,256]{1,0:T(8,128)(2,1)} %split.17), channel_id=1, source_target_pairs={{4,0},{8,12},{5,1},{9,13},{6,2},{10,14},{7,3},{11,15},{20,16},{24,... | collective-permute-start | bytes 5505032 | tf_op jit(solution)/shard_map/ppermute | solution.py:201
  (19 other events, 433.1 us)
Sparse Core Ops, SparseCore 0:
  107.1 19.4 all-gather.4
  189.7 19.4 all-gather.2

commit v2 on v0

--- a/solution.py
+++ b/solution.py
@@ -93,7 +93,167 @@
     return (token_grad.astype(jnp.bfloat16), up_grad, down_grad, gain_grad, inner[:, 0])
 
 
+def swap(value, axis):
+    return lax.ppermute(value, axis, ((0, 1), (1, 0)))
+
+
+def tie(*values):
+    return lax.optimization_barrier(values)
+
+
+def rounded(value):
+    return value.astype(jnp.bfloat16)
+
+
+def local_line(
+    tokens, cotangent, norm_gain, expert_ids, combine_weight, up_weight, down_weight
+):
+    count, piece = tokens.shape
+    width = piece * 2
+    capacity = count * 5 // 8
+    inward, middle, outward = ((0, 1), (3, 2)), ((1, 2), (2, 1)), ((1, 0), (2, 3))
+    place = lax.axis_index("expert")
+    mine = place // 2
+    is_inner = (place == 1) | (place == 2)
+    part = lax.axis_index("parts")
+    side = lax.axis_index("tensor")
+
+    def along(value, pairs):
+        return lax.ppermute(value, "expert", pairs)
+
+    def half(weight):
+        size = weight.shape[0] // 2
+        return lax.dynamic_slice_in_dim(weight, part * size, size, 0)
+
+    tokens_in = along(tokens, inward)
+    up_own = lax.all_gather(up_weight, "tensor", axis=1, tiled=True)
+    down_own = lax.all_gather(down_weight, "tensor", axis=0, tiled=True)
+    token_f = tokens.astype(jnp.float32)
+    squares = lax.psum(jnp.sum(token_f * token_f, axis=1), "dp")
+    scale = lax.rsqrt(squares / width + 1e-06)
+    small = jnp.stack([scale, combine_weight, expert_ids[:, 0].astype(jnp.float32)])
+    small_in = along(small, inward)
+
+    def places(facts, expert):
+        hit = facts[2].astype(jnp.int32) == expert
+        slot = jnp.where(hit, jnp.cumsum(hit.astype(jnp.int32)) - 1, -1)
+        return rounded(slot[:, None] == jnp.arange(capacity, dtype=jnp.int32)[None, :])
+
+    def normed_of(block, facts):
+        return rounded(block.astype(jnp.float32) * facts[0][:, None] * norm_gain[None, :])
+
+    def scaled_of(block, facts):
+        return rounded(facts[1][:, None] * block.astype(jnp.float32))
+
+    def picked(where, rows):
+        return rounded(contract(where, rows, 0, 0))
+
+    keep_a, send_a = places(small, mine), places(small, 1 - mine)
+    normed_a, scaled_a = normed_of(tokens, small), scaled_of(cotangent, small)
+    far_xa = along(picked(send_a, normed_a), middle)
+    near_xa, near_da = picked(keep_a, normed_a), picked(keep_a, scaled_a)
+    send_da = picked(send_a, scaled_a)
+    half_up, tokens_in, far_xa, send_da, near_xa, near_da, small_in = tie(
+        half(up_weight), tokens_in, far_xa, send_da, near_xa, near_da, small_in
+    )
+
+    up_in = along(half_up, inward)
+    far_da = along(send_da, middle)
+    keep_b, send_b = places(small_in, mine), places(small_in, 1 - mine)
+    normed_b = normed_of(tokens_in, small_in)
+    send_xb, near_xb = picked(send_b, normed_b), picked(keep_b, normed_b)
+    half_down, up_in, far_da, send_xb, near_xb = tie(
+        half(down_weight), up_in, far_da, send_xb, near_xb
+    )
+
+    down_in = along(half_down, inward)
+    far_xb = along(send_xb, middle)
+    up_out = lax.all_gather(up_in, "parts", axis=0, tiled=True)
+    cot_sent, down_in, far_xb, up_out = tie(cotangent, down_in, far_xb, up_out)
+
+    cotangent_in = along(cot_sent, inward)
+    up_out = lax.all_gather(up_out, "tensor", axis=1, tiled=True)
+    down_out = lax.all_gather(down_in, "parts", axis=0, tiled=True)
+    down_out = lax.all_gather(down_out, "tensor", axis=0, tiled=True)
+    rows_x = jnp.concatenate([far_xa, near_xa, near_xb, far_xb])
+
+    def over_dp(value):
+        return value.astype(jnp.float32) + swap(value, "dp").astype(jnp.float32)
+
+    pre_own = rounded(contract(rows_x, up_own, 1, 0))
+    pre_out = rounded(contract(rows_x, up_out, 1, 0))
+    pre = jnp.concatenate([over_dp(pre_own), over_dp(pre_out)], axis=1)
+    cotangent_in, pre_out, down_out = tie(cotangent_in, pre_out, down_out)
+
+    scaled_b = scaled_of(cotangent_in, small_in)
+    far_db = along(picked(send_b, scaled_b), middle)
+    early = jnp.concatenate([far_da, near_da, picked(keep_b, scaled_b)])
+
+    def back_of(rows):
+        parts_of = [contract(rows, down_own, 1, 1), contract(rows, down_out, 1, 1)]
+        return over_dp(rounded(jnp.concatenate(parts_of, axis=1)))
+
+    back = jnp.concatenate([back_of(early), back_of(far_db)])
+    rows_d = jnp.concatenate([early, far_db])
+    act = rounded(jax.nn.silu(pre))
+    dpre = rounded(back * slope(pre))
+    unit = act.shape[1] // 2
+
+    def row_grad(rows):
+        own = contract(rows[:, :unit], up_own, 1, 1)
+        return rounded(own + contract(rows[:, unit:], up_out, 1, 1))
+
+    back_b = along(row_grad(dpre[3 * capacity :]), middle)
+    back_a = along(row_grad(dpre[:capacity]), middle)
+    near_grad = row_grad(dpre[capacity : 3 * capacity])
+
+    def shared(terms, axis):
+        size = terms.shape[axis] // 2
+        own = lax.dynamic_slice_in_dim(terms, side * size, size, axis)
+        other = lax.dynamic_slice_in_dim(terms, (1 - side) * size, size, axis)
+        return rounded(own + swap(rounded(other), "tensor").astype(jnp.float32))
+
+    down_far = along(shared(contract(act[:, unit:], rows_d, 0, 0), 0), outward)
+    up_far = along(shared(contract(rows_x, dpre[:, unit:], 0, 0), 1), outward)
+    down_near = shared(contract(act[:, :unit], rows_d, 0, 0), 0)
+    up_near = shared(contract(rows_x, dpre[:, :unit], 0, 0), 1)
+
+    def restored(keep, near, send, far):
+        return rounded(contract(keep, near, 1, 0) + contract(send, far, 1, 0))
+
+    grad_b = restored(keep_b, near_grad[capacity:], send_b, back_b)
+    grad_in = along(grad_b, outward)
+    grad_a = restored(keep_a, near_grad[:capacity], send_a, back_a)
+
+    def gain_of(grad, block, facts):
+        block = block.astype(jnp.float32) * facts[0][:, None]
+        return jnp.sum(grad.astype(jnp.float32) * block, axis=0)
+
+    def inner_of(grad, block):
+        gained = block.astype(jnp.float32) * norm_gain[None, :]
+        return jnp.sum(gained * grad.astype(jnp.float32), axis=1)
+
+    gain_terms = gain_of(grad_a, tokens, small) + gain_of(grad_b, tokens_in, small_in)
+    gain_grad = lax.psum(jnp.where(is_inner, gain_terms, 0.0), ("expert", "tensor"))
+    inner_ab = jnp.stack([inner_of(grad_a, tokens), inner_of(grad_b, tokens_in)])
+    inner_ab = over_dp(inner_ab)
+    inner = jnp.where(is_inner, inner_ab[0], along(inner_ab[1], outward))
+    normed_grad = jnp.where(is_inner, grad_a, grad_in).astype(jnp.float32)
+    scale = scale[:, None]
+    cubed = scale * scale * scale
+    token_grad = (
+        cotangent.astype(jnp.float32)
+        + scale * norm_gain[None, :] * normed_grad
+        - token_f * cubed * inner[:, None] / width
+    )
+    up_grad = jnp.where(is_inner, up_near, up_far)
+    down_grad = jnp.where(is_inner, down_near, down_far)
+    return (rounded(token_grad), up_grad, down_grad, gain_grad, inner)
+
+
 def solution(mesh):
+    sizes = tuple(mesh.shape[name] for name in ("parts", "expert", "dp", "tensor"))
+    body = local_line if sizes == (2, 4, 2, 2) else local
     in_specs = (
         P(("parts", "expert", "tensor"), "dp"),
         P(("parts", "expert", "tensor"), "dp"),
@@ -110,4 +270,4 @@
         P(("parts", "dp")),
         P(("parts", "expert", "tensor")),
     )
-    return jax.shard_map(local, mesh=mesh, in_specs=in_specs, out_specs=out_specs, check_vma=False)
+    return jax.shard_map(body, mesh=mesh, in_specs=in_specs, out_specs=out_specs, check_vma=False)

time: 470 us -> 485 us (1.032); the launches traced: 470 us -> 477 us
  waiting for transfers between devices: 328 us -> 218 us
  matrix products: 39.9 us -> 86.6 us
  starting transfers between devices: 16.7 us -> 54.2 us
  blocking collectives: 36.4 us -> 53.7 us
  other arithmetic: 18.6 us -> 26.5 us
  local copies, waits for them, and re-layouts: 15.6 us -> 22.7 us
    all_to_all x3 -> x0, waiting for transfers between devices: 273 us -> none  [the longest x1 94.9 us: local(): lax.all_to_all(row_grad.reshape(n_expert, capacity, piece), 'expert', spl...]
    ppermute x0 -> x24, waiting for transfers between devices: none -> 177 us  [the longest x15 140 us: along(): return lax.ppermute(value, 'expert', pairs)]
    ppermute x0 -> x24, starting transfers between devices: none -> 54 us  [the longest x15 45.5 us: along(): return lax.ppermute(value, 'expert', pairs)]
    dot_general x6 -> x28, matrix products: 33.1 us -> 86.6 us  [contract(): lax.dot_general(left, right, (((left_dim,), (right_dim,)), ((), ())), pre...]
    psum x1 -> x0, waiting for transfers between devices: 45.2 us -> none  [local(): lax.psum(up_part.astype(jnp.bfloat16), 'dp').astype(jnp.float32)]
    all_gather x2 -> x6, waiting for transfers between devices: 8.53 us -> 38.9 us  [the longest x1 30.4 us: local_line(): down_out = lax.all_gather(down_in, 'parts', axis=0, tiled=True)]
    psum x3 -> x2, blocking collectives: 36.4 us -> 53.7 us  [the longest x1 48.7 us: local_line(): lax.psum(jnp.where(is_inner, gain_terms, 0.0), ('expert', 'tensor'))]
    all_to_all x3 -> x0, starting transfers between devices: 16.4 us -> none  [the longest x1 6.45 us: local(): lax.all_to_all(outward(packed_d), 'expert', split_axis=0, concat_axis=0,...]
  transfers between devices with their start and end apart: 8 -> 30, of which waited for: 5 -> 13; matrix products, arithmetic and copies ran while one was open for 11% -> 23% of each run, Pallas kernels for 0% -> 0%
where the time goes in v2:
time: 485 us; the launch traced here: 477 us
  waiting for transfers between devices  218 us (45%)
  matrix products  86.6 us (18%)
  starting transfers between devices  54.2 us (11%)
  blocking collectives  53.7 us (11%)
  other arithmetic  26.5 us (5%)
  local copies, waits for them, and re-layouts  22.7 us (5%)
  between operations  15.1 us (3%)
    ppermute x15, waiting for transfers between devices, along(): return lax.ppermute(value, 'expert', pairs)  140 us
    dot_general x28, matrix products, contract(): lax.dot_general(left, right, (((left_dim,), (right_dim,)), ((), ())), pre...  86.6 us
    psum x1, blocking collectives, local_line(): lax.psum(jnp.where(is_inner, gain_terms, 0.0), ('expert', 'tensor'))  48.7 us
    ppermute x15, starting transfers between devices, along(): return lax.ppermute(value, 'expert', pairs)  45.5 us
    ppermute x9, waiting for transfers between devices, swap(): return lax.ppermute(value, axis, ((0, 1), (1, 0)))  37.8 us
    all_gather x1, waiting for transfers between devices, local_line(): down_out = lax.all_gather(down_in, 'parts', axis=0, tiled=True)  30.4 us
    unnamed x67, local copies, waits for them, and re-layouts  11.7 us
    convert_element_type x4, other arithmetic, rounded(): return value.astype(jnp.bfloat16)  10.6 us
  transfers between devices with their start and end apart: 30, of which 13 were waited for; matrix products, arithmetic and copies ran while one was open for 23% of the time, Pallas kernels for 0%

profile of v2, /device:TPU:0, one launch (start us, length us, event | category | flops | bytes accessed | tf_op | source)
XLA Modules:
  0.0 476.8 jit_solution(16240390256191865301)
XLA Ops:
  7.2 6.3 %collective-permute-start = (bf16[256,3584]{1,0:T(8,128)(2,1)}, bf16[256,3584]{1,0:T(8,128)(2,1)}, u32[]{:S(2)}, u32[]{:S(2)}) collective-permute-start(bf16[256,3584]{1,0:T(8,128)(2,1)} %param.7), channel_id=1, source_target_pairs={{0,4},{12,8},{1,5},{13,9},{2,6},{14,10},{3,7},{15,11},{16,20},{28,... | collective-permute-start | bytes 5505032 | tf_op jit(solution)/shard_map/ppermute | solution.py:122
  15.5 4.9 %psum.14 = f32[256]{0:T(256)S(1)} all-reduce(f32[256]{0:T(256)S(1)} %fusion.16), channel_id=1, replica_groups=mesh['parts'=2,'expert'=4,'dp'=2,'tensor'=2] {'dp'}, use_global_device_ids=true, to_apply=%region_1.2 | all-reduce | flops 256 | bytes 2048 | tf_op jit(solution)/shard_map/psum | solution.py:132
  38.9 13.0 %collective-permute-done.2 = f32[3,256]{1,0:T(4,128)S(1)} collective-permute-done((f32[3,256]{1,0:T(4,128)S(1)}, f32[3,256]{1,0:T(4,128)S(1)}, u32[]{:S(2)}, u32[]{:S(2)}) %collective-permute-start.2) | collective-permute-done | bytes 3104 | tf_op jit(solution)/shard_map/ppermute | solution.py:122
  51.9 5.3 %collective-permute-start.3 = (bf16[1792,256]{1,0:T(8,128)(2,1)}, bf16[1792,256]{1,0:T(8,128)(2,1)}, u32[]{:S(2)}, u32[]{:S(2)}) collective-permute-start(bf16[1792,256]{1,0:T(8,128)(2,1)} %constant_dynamic-slice_fusion), channel_id=1, source_target_pairs={{0,4},{12,8},{1,5},{13,9},{2,6},{14,10},{3,7},{15,11},{16,20},{28,... | collective-permute-start | bytes 2752520 | tf_op jit(solution)/shard_map/ppermute | solution.py:122
  66.7 8.7 %collective-permute-done.3 = bf16[1792,256]{1,0:T(8,128)(2,1)} collective-permute-done((bf16[1792,256]{1,0:T(8,128)(2,1)}, bf16[1792,256]{1,0:T(8,128)(2,1)}, u32[]{:S(2)}, u32[]{:S(2)}) %collective-permute-start.3) | collective-permute-done | bytes 917536 | tf_op jit(solution)/shard_map/ppermute | solution.py:122
  76.2 14.1 %collective-permute-start.5 = (bf16[128,3584]{1,0:T(8,128)(2,1)}, bf16[128,3584]{1,0:T(8,128)(2,1)}, u32[]{:S(2)}, u32[]{:S(2)}) collective-permute-start(bf16[128,3584]{1,0:T(8,128)(2,1)} %constant_dynamic-slice_fusion.1), channel_id=1, source_target_pairs={{0,4},{12,8},{1,5},{13,9},{2,6},{14,10},{3,7},{15,11},{16,20},{28,... | collective-permute-start | bytes 2752520 | tf_op jit(solution)/shard_map/ppermute | solution.py:122
  90.3 16.9 %collective-permute-done.5 = bf16[128,3584]{1,0:T(8,128)(2,1)} collective-permute-done((bf16[128,3584]{1,0:T(8,128)(2,1)}, bf16[128,3584]{1,0:T(8,128)(2,1)}, u32[]{:S(2)}, u32[]{:S(2)}) %collective-permute-start.5) | collective-permute-done | bytes 917536 | tf_op jit(solution)/shard_map/ppermute | solution.py:122
  107.2 5.6 %all-gather.7.cloned.1.call-done = bf16[3584,256]{1,0:T(8,128)(2,1)} async-done(((bf16[1792,256]{1,0:T(8,128)(2,1)}), bf16[3584,256]{1,0:T(8,128)(2,1)}) %all-gather.7.cloned.1.call-update) | async-done | bytes 1835024 | tf_op jit(solution)/shard_map/all_gather | solution.py:171
  114.3 30.4 %all-gather.11.cloned.1.call-done = bf16[256,3584]{1,0:T(8,128)(2,1)} async-done(((bf16[128,3584]{1,0:T(8,128)(2,1)}), bf16[256,3584]{1,0:T(8,128)(2,1)}) %all-gather.11.cloned.1.call-update) | async-done | bytes 1835024 | tf_op jit(solution)/shard_map/all_gather | solution.py:176
  149.9 4.7 collective-permute-start.7
  158.5 6.0 %convolution_convert_fusion.8 = bf16[640,512]{1,0:T(8,128)(2,1)S(1)} fusion(bf16[640,3584]{1,0:T(8,128)(2,1)} %constant_dynamic-update-slice_fusion, bf16[3584,512]{1,0:T(8,128)(2,1)} %all-gather.17.cloned.1.call-done), kind=kOutput, calls=%fused_computation.65 | convolution fusion | flops 2349137920 | bytes 8912896 | tf_op jit(solution)/shard_map/dot_general | solution.py:13
  166.3 15.3 %collective-permute-done.11 = bf16[640,512]{1,0:T(8,128)(2,1)} collective-permute-done((bf16[640,512]{1,0:T(8,128)(2,1)S(1)}, bf16[640,512]{1,0:T(8,128)(2,1)}, u32[]{:S(2)}, u32[]{:S(2)}) %collective-permute-start.11) | collective-permute-done | bytes 655392 | tf_op jit(solution)/shard_map/ppermute | solution.py:97
  183.2 7.9 %convolution_convert_fusion.9 = bf16[640,512]{1,0:T(8,128)(2,1)} fusion(bf16[640,3584]{1,0:T(8,128)(2,1)} %constant_dynamic-update-slice_fusion, bf16[3584,512]{1,0:T(8,128)(2,1)} %all-gather.9.cloned.1.call-done), kind=kOutput, calls=%fused_computation.66 | convolution fusion | flops 2349137920 | bytes 8912896 | tf_op jit(solution)/shard_map/dot_general | solution.py:13
  205.6 5.2 %fusion.24 = bf16[480,512]{1,0:T(8,128)(2,1)S(1)} fusion(bf16[512,3584]{1,0:T(8,128)(2,1)} %all-gather.15.cloned.1.call-done, bf16[160,3584]{1,0:T(8,128)(2,1)} %copy-done.18, bf16[160,3584]{1,0:T(8,128)(2,1)} %convolution_convert_fusion.4, bf16[160,3584]{1,0:T(8,128)(2,1)} %collective-permute-done.4), kind=kOutput, calls=%fused_computation.69 | convolution fusion | flops 1772175360 | bytes 7602176 | tf_op jit(solution)/shard_map/dot_general | solution.py:13
  219.9 15.9 %collective-permute-done.8 = bf16[480,1024]{1,0:T(8,128)(2,1)S(1)} collective-permute-done((bf16[480,1024]{1,0:T(8,128)(2,1)S(1)}, bf16[480,1024]{1,0:T(8,128)(2,1)S(1)}, u32[]{:S(2)}, u32[]{:S(2)}) %collective-permute-start.8) | collective-permute-done | bytes 983072 | tf_op jit(solution)/shard_map/ppermute | solution.py:97
  236.0 4.8 %collective-permute-done.10 = bf16[160,1024]{1,0:T(8,128)(2,1)S(1)} collective-permute-done((bf16[160,1024]{1,0:T(8,128)(2,1)S(1)}, bf16[160,1024]{1,0:T(8,128)(2,1)S(1)}, u32[]{:S(2)}, u32[]{:S(2)}) %collective-permute-start.10) | collective-permute-done | bytes 327712 | tf_op jit(solution)/shard_map/ppermute | solution.py:97
  242.1 5.0 %fusion.36 = f32[3584,512]{1,0:T(8,128)S(1)} fusion(bf16[640,3584]{1,0:T(8,128)(2,1)} %constant_dynamic-update-slice_fusion, bf16[640,1024]{1,0:T(8,128)(2,1)S(1)} %get-tuple-element.48), kind=kOutput, calls=%fused_computation.82 | convolution fusion | flops 2348810240 | bytes 12582912 | tf_op jit(solution)/shard_map/dot_general | solution.py:13
  247.1 6.8 %fusion.38 = f32[3584,512]{1,0:T(8,128)S(1)} fusion(bf16[640,3584]{1,0:T(8,128)(2,1)} %constant_dynamic-update-slice_fusion, bf16[640,1024]{1,0:T(8,128)(2,1)S(1)} %get-tuple-element.48), kind=kOutput, calls=%fused_computation.84 | convolution fusion | flops 2348810240 | bytes 12582912 | tf_op jit(solution)/shard_map/dot_general | solution.py:13
  277.6 4.6 fusion.31
  288.2 5.5 %fusion.13 = (f32[3584]{0:T(1024)S(1)}, f32[256]{0:T(256)S(1)}, f32[256]{0:T(256)S(1)}, f32[3584]{0:T(1024)S(1)}, bf16[256,3584]{1,0:T(8,128)(2,1)}) fusion(bf16[256,3584]{1,0:T(8,128)(2,1)S(1)} %copy-done.3, f32[256]{0:T(256)S(1)} %get-tuple-element.60, f32[3584]{0:T(1024)S(1)} %copy-done.25, f32[256]{0:T(256)S(1)} %bitcast.69, ...), kind=kOutput, calls=%fused_computation.39 | convolution fusion | flops 310149632 | bytes 12205056 | tf_op jit(solution)/shard_map/dot_general | solution.py:13
  298.7 48.7 %psum.15 = f32[3584]{0:T(1024)} all-reduce(f32[3584]{0:T(1024)S(1)} %add_select_fusion), channel_id=1, replica_groups=mesh['parts'=2,'expert'=4,'dp'=2,'tensor'=2] {'expert','tensor'}, use_global_device_ids=true, to_apply=%region_14.15 | all-reduce | flops 3584 | bytes 28672 | tf_op jit(solution)/shard_map/psum | solution.py:237
  358.3 34.2 %collective-permute-done.15 = bf16[256,3584]{1,0:T(8,128)(2,1)S(1)} collective-permute-done((bf16[256,3584]{1,0:T(8,128)(2,1)}, bf16[256,3584]{1,0:T(8,128)(2,1)S(1)}, u32[]{:S(2)}, u32[]{:S(2)}) %collective-permute-start.15) | collective-permute-done | bytes 1835040 | tf_op jit(solution)/shard_map/ppermute | solution.py:122
  395.6 36.2 %collective-permute-done.20 = bf16[3584,256]{1,0:T(8,128)(2,1)S(1)} collective-permute-done((bf16[3584,256]{1,0:T(8,128)(2,1)S(1)}, bf16[3584,256]{1,0:T(8,128)(2,1)S(1)}, u32[]{:S(2)}, u32[]{:S(2)}) %collective-permute-start.20) | collective-permute-done | bytes 1835040 | tf_op jit(solution)/shard_map/ppermute | solution.py:122
  435.5 30.5 %collective-permute-done.23 = bf16[256,3584]{1,0:T(8,128)(2,1)S(1)} collective-permute-done((bf16[256,3584]{1,0:T(8,128)(2,1)S(1)}, bf16[256,3584]{1,0:T(8,128)(2,1)S(1)}, u32[]{:S(2)}, u32[]{:S(2)}) %collective-permute-start.23) | collective-permute-done | bytes 1835040 | tf_op jit(solution)/shard_map/ppermute | solution.py:122
  (191 shorter events, 125.1 us)
Async XLA Ops:
  7.2 105.7 %all-gather.7.cloned.1.call-start = ((), (), s32[]{:S(2)}) async-start(), calls=%async_computation | async-start | bytes 2752512 | tf_op jit(solution)/shard_map/all_gather | solution.py:171
  7.2 44.7 %collective-permute-start = (bf16[256,3584]{1,0:T(8,128)(2,1)}, bf16[256,3584]{1,0:T(8,128)(2,1)}, u32[]{:S(2)}, u32[]{:S(2)}) collective-permute-start(bf16[256,3584]{1,0:T(8,128)(2,1)} %param.7), channel_id=1, source_target_pairs={{0,4},{12,8},{1,5},{13,9},{2,6},{14,10},{3,7},{15,11},{16,20},{28,... | collective-permute-start | bytes 5505032 | tf_op jit(solution)/shard_map/ppermute | solution.py:122
  26.3 25.6 %collective-permute-start.1 = (bf16[160,3584]{1,0:T(8,128)(2,1)}, bf16[160,3584]{1,0:T(8,128)(2,1)}, u32[]{:S(2)}, u32[]{:S(2)}) collective-permute-start(bf16[160,3584]{1,0:T(8,128)(2,1)} %convolution_convert_fusion.7), channel_id=1, source_target_pairs={{4,8},{8,4},{5,9},{9,5},{6,10},{10,6},{7,11},{11,7},{20,24},{24,20... | collective-permute-start | bytes 3440648 | tf_op jit(solution)/shard_map/ppermute | solution.py:122
  28.1 23.9 %collective-permute-start.2 = (f32[3,256]{1,0:T(4,128)S(1)}, f32[3,256]{1,0:T(4,128)S(1)}, u32[]{:S(2)}, u32[]{:S(2)}) collective-permute-start(f32[3,256]{1,0:T(4,128)S(1)} %pad_maximum_fusion.13), channel_id=1, source_target_pairs={{0,4},{12,8},{1,5},{13,9},{2,6},{14,10},{3,7},{15,11},{16,20},{28,... | collective-permute-start | bytes 9224 | tf_op jit(solution)/shard_map/ppermute | solution.py:122
  75.4 69.2 %all-gather.11.cloned.1.call-start = ((), (), s32[]{:S(2)}) async-start(), calls=%async_computation.2 | async-start | bytes 2752512 | tf_op jit(solution)/shard_map/all_gather | solution.py:176
  75.5 31.8 %collective-permute-start.6 = (bf16[160,3584]{1,0:T(8,128)(2,1)}, bf16[160,3584]{1,0:T(8,128)(2,1)S(1)}, u32[]{:S(2)}, u32[]{:S(2)}) collective-permute-start(bf16[160,3584]{1,0:T(8,128)(2,1)} %convolution_convert_fusion.3), channel_id=1, source_target_pairs={{4,8},{8,4},{5,9},{9,5},{6,10},{10,6},{7,11},{11,7},{20,24},{24,20... | collective-permute-start | bytes 3440648 | tf_op jit(solution)/shard_map/ppermute | solution.py:122
  76.2 31.0 %collective-permute-start.5 = (bf16[128,3584]{1,0:T(8,128)(2,1)}, bf16[128,3584]{1,0:T(8,128)(2,1)}, u32[]{:S(2)}, u32[]{:S(2)}) collective-permute-start(bf16[128,3584]{1,0:T(8,128)(2,1)} %constant_dynamic-slice_fusion.1), channel_id=1, source_target_pairs={{0,4},{12,8},{1,5},{13,9},{2,6},{14,10},{3,7},{15,11},{16,20},{28,... | collective-permute-start | bytes 2752520 | tf_op jit(solution)/shard_map/ppermute | solution.py:122
  112.9 45.6 %all-gather.17.cloned.1.call-start = ((), (), s32[]{:S(2)}) async-start(), calls=%async_computation.5 | async-start | bytes 5505024 | tf_op jit(solution)/shard_map/all_gather | solution.py:129
  113.6 69.6 %all-gather.9.cloned.1.call-start = ((), (), s32[]{:S(2)}) async-start(), calls=%async_computation.1 | async-start | bytes 5505024 | tf_op jit(solution)/shard_map/all_gather | solution.py:175
  114.2 78.8 %all-gather.13.cloned.1.call-start = ((), (), s32[]{:S(2)}) async-start(), calls=%async_computation.3 | async-start | bytes 5505024 | tf_op jit(solution)/shard_map/all_gather | solution.py:177
  144.7 61.0 %all-gather.15.cloned.1.call-start = ((), (), s32[]{:S(2)}) async-start(), calls=%async_computation.4 | async-start | bytes 5505024 | tf_op jit(solution)/shard_map/all_gather | solution.py:130
  149.9 43.1 %collective-permute-start.7 = (bf16[256,3584]{1,0:T(8,128)(2,1)S(1)}, bf16[256,3584]{1,0:T(8,128)(2,1)}, u32[]{:S(2)}, u32[]{:S(2)}) collective-permute-start(bf16[256,3584]{1,0:T(8,128)(2,1)S(1)} %copy-done.2), channel_id=1, source_target_pairs={{0,4},{12,8},{1,5},{13,9},{2,6},{14,10},{3,7},{15,11},{16,20},{28,... | collective-permute-start | bytes 5505032 | tf_op jit(solution)/shard_map/ppermute | solution.py:122
  191.2 27.2 %collective-permute-start.12 = (bf16[640,512]{1,0:T(8,128)(2,1)}, bf16[640,512]{1,0:T(8,128)(2,1)}, u32[]{:S(2)}, u32[]{:S(2)}) collective-permute-start(bf16[640,512]{1,0:T(8,128)(2,1)} %convolution_convert_fusion.9), channel_id=1, source_target_pairs={{0,2},{2,0},{1,3},{3,1},{4,6},{6,4},{5,7},{7,5},{8,10},{10,8},{9,1... | collective-permute-start | bytes 1966088 | tf_op jit(solution)/shard_map/ppermute | solution.py:97
  211.0 24.8 %collective-permute-start.8 = (bf16[480,1024]{1,0:T(8,128)(2,1)S(1)}, bf16[480,1024]{1,0:T(8,128)(2,1)S(1)}, u32[]{:S(2)}, u32[]{:S(2)}) collective-permute-start(bf16[480,1024]{1,0:T(8,128)(2,1)S(1)} %pad_maximum_fusion.9), channel_id=1, source_target_pairs={{0,2},{2,0},{1,3},{3,1},{4,6},{6,4},{5,7},{7,5},{8,10},{10,8},{9,1... | collective-permute-start | bytes 2949128 | tf_op jit(solution)/shard_map/ppermute | solution.py:97
  260.0 26.7 %collective-permute-start.14 = (bf16[160,3584]{1,0:T(8,128)(2,1)S(1)}, bf16[160,3584]{1,0:T(8,128)(2,1)S(1)}, u32[]{:S(2)}, u32[]{:S(2)}) collective-permute-start(bf16[160,3584]{1,0:T(8,128)(2,1)S(1)} %fusion.4), channel_id=1, source_target_pairs={{4,8},{8,4},{5,9},{9,5},{6,10},{10,6},{7,11},{11,7},{20,24},{24,20... | collective-permute-start | bytes 3440648 | tf_op jit(solution)/shard_map/ppermute | solution.py:122
  263.5 24.5 %collective-permute-start.13 = (bf16[160,3584]{1,0:T(8,128)(2,1)S(1)}, bf16[160,3584]{1,0:T(8,128)(2,1)S(1)}, u32[]{:S(2)}, u32[]{:S(2)}) collective-permute-start(bf16[160,3584]{1,0:T(8,128)(2,1)S(1)} %fusion.3), channel_id=1, source_target_pairs={{4,8},{8,4},{5,9},{9,5},{6,10},{10,6},{7,11},{11,7},{20,24},{24,20... | collective-permute-start | bytes 3440648 | tf_op jit(solution)/shard_map/ppermute | solution.py:122
  265.9 82.9 %collective-permute-start.19 = (bf16[3584,256]{1,0:T(8,128)(2,1)}, bf16[3584,256]{1,0:T(8,128)(2,1)}, u32[]{:S(2)}, u32[]{:S(2)}) collective-permute-start(bf16[3584,256]{1,0:T(8,128)(2,1)} %dynamic-slice_convert_fusion.2), channel_id=1, source_target_pairs={{0,1},{1,0},{2,3},{3,2},{4,5},{5,4},{6,7},{7,6},{8,9},{9,8},{10,11... | collective-permute-start | bytes 5505032 | tf_op jit(solution)/shard_map/ppermute | solution.py:97
  267.4 128.2 %collective-permute-start.18 = (bf16[3584,256]{1,0:T(8,128)(2,1)}, bf16[3584,256]{1,0:T(8,128)(2,1)}, u32[]{:S(2)}, u32[]{:S(2)}) collective-permute-start(bf16[3584,256]{1,0:T(8,128)(2,1)} %dynamic-slice_convert_fusion.3), channel_id=1, source_target_pairs={{0,1},{1,0},{2,3},{3,2},{4,5},{5,4},{6,7},{7,6},{8,9},{9,8},{10,11... | collective-permute-start | bytes 5505032 | tf_op jit(solution)/shard_map/ppermute | solution.py:97
  276.2 77.4 %collective-permute-start.22 = (bf16[256,3584]{1,0:T(8,128)(2,1)}, bf16[256,3584]{1,0:T(8,128)(2,1)}, u32[]{:S(2)}, u32[]{:S(2)}) collective-permute-start(bf16[256,3584]{1,0:T(8,128)(2,1)} %dynamic-slice_convert_fusion), channel_id=1, source_target_pairs={{0,1},{1,0},{2,3},{3,2},{4,5},{5,4},{6,7},{7,6},{8,9},{9,8},{10,11... | collective-permute-start | bytes 5505032 | tf_op jit(solution)/shard_map/ppermute | solution.py:97
  286.7 148.8 %collective-permute-start.21 = (bf16[256,3584]{1,0:T(8,128)(2,1)}, bf16[256,3584]{1,0:T(8,128)(2,1)}, u32[]{:S(2)}, u32[]{:S(2)}) collective-permute-start(bf16[256,3584]{1,0:T(8,128)(2,1)} %dynamic-slice_convert_fusion.1), channel_id=1, source_target_pairs={{0,1},{1,0},{2,3},{3,2},{4,5},{5,4},{6,7},{7,6},{8,9},{9,8},{10,11... | collective-permute-start | bytes 5505032 | tf_op jit(solution)/shard_map/ppermute | solution.py:97
  297.4 50.0 %collective-permute-start.17 = (f32[256]{0:T(256)S(1)}, f32[256]{0:T(256)S(1)}, u32[]{:S(2)}, u32[]{:S(2)}) collective-permute-start(f32[256]{0:T(256)S(1)} %bitcast.70), channel_id=1, source_target_pairs={{4,0},{8,12},{5,1},{9,13},{6,2},{10,14},{7,3},{11,15},{20,16},{24,... | collective-permute-start | bytes 3080 | tf_op jit(solution)/shard_map/ppermute | solution.py:122
  347.5 45.0 %collective-permute-start.15 = (bf16[256,3584]{1,0:T(8,128)(2,1)}, bf16[256,3584]{1,0:T(8,128)(2,1)S(1)}, u32[]{:S(2)}, u32[]{:S(2)}) collective-permute-start(bf16[256,3584]{1,0:T(8,128)(2,1)} %copy-done.14), channel_id=1, source_target_pairs={{4,0},{8,12},{5,1},{9,13},{6,2},{10,14},{7,3},{11,15},{20,16},{24,... | collective-permute-start | bytes 5505032 | tf_op jit(solution)/shard_map/ppermute | solution.py:122
  352.0 79.8 %collective-permute-start.20 = (bf16[3584,256]{1,0:T(8,128)(2,1)S(1)}, bf16[3584,256]{1,0:T(8,128)(2,1)S(1)}, u32[]{:S(2)}, u32[]{:S(2)}) collective-permute-start(bf16[3584,256]{1,0:T(8,128)(2,1)S(1)} %add_convert_fusion.2), channel_id=1, source_target_pairs={{4,0},{8,12},{5,1},{9,13},{6,2},{10,14},{7,3},{11,15},{20,16},{24,... | collective-permute-start | bytes 5505032 | tf_op jit(solution)/shard_map/ppermute | solution.py:122
  356.8 109.2 %collective-permute-start.23 = (bf16[256,3584]{1,0:T(8,128)(2,1)S(1)}, bf16[256,3584]{1,0:T(8,128)(2,1)S(1)}, u32[]{:S(2)}, u32[]{:S(2)}) collective-permute-start(bf16[256,3584]{1,0:T(8,128)(2,1)S(1)} %add_convert_fusion), channel_id=1, source_target_pairs={{4,0},{8,12},{5,1},{9,13},{6,2},{10,14},{7,3},{11,15},{20,16},{24,... | collective-permute-start | bytes 5505032 | tf_op jit(solution)/shard_map/ppermute | solution.py:122
  (38 other events, 732.7 us)
Sparse Core Ops, SparseCore 0:
  75.5 37.2 all-gather.6
  114.4 30.1 all-gather.10
  146.2 12.3 all-gather.16
  159.9 13.5 all-gather.8
  174.8 14.0 all-gather.12
  190.4 14.0 all-gather.14
